TPU v7x, 32 devices: a whole 2x2x4 slice. The times are simulated.
32 devices in a mesh: wide: 8 (over y, x, core), narrow: 4 (over z).
Axes of the slice: x: 2, y: 2, z: 4, core: 2. Of those that a mesh axis runs over, the one named last changes fastest.
Arguments:
- old_field: float32 [1024, 128, 128], P(('wide', 'narrow')), may hold values from -6 to 6
- old_level: int32 [1024], P(('wide', 'narrow')), may hold values from 0 to 1
- new_source: int32 [16, 16], P('wide', 'narrow'), may hold values from 0 to 1023, as said below
- stretch_coef: float32 [4096, 4096], P('wide', 'narrow'), may hold values from 0.2 to 2
- bend_coef: float32 [4096, 4096], P('wide', 'narrow'), may hold values from 0.05 to 0.5
- load_field: float32 [4096, 4096], P('wide', 'narrow'), may hold values from -6 to 6
Outputs:
- relaxed: float32 [4096, 4096], P('wide', 'narrow')
Inputs may be any that keep to these rules, and one draw needn't show every extreme that they name: new_source names an old block held by a device with the same narrow index; one old device gives at most 2 sibling groups to one new device, and exactly 2 wherever it gives any.
All inputs are finite; a program needn't handle non-finite values.
Results may differ from a plain program's by a relative error of at most 0.0001.
Values sent between devices are 32-bit elements; how exact they have to be, the bound alone decides.
A program may use at most 128 MiB of HBM per device.

v0:
```python
import jax
import jax.numpy as jnp
from jax import lax
from jax.sharding import PartitionSpec as P

SWEEPS = 2


OMEGA = 0.5


def padded_2(cells, sides, width):
    for axis, dim in sides:
        count = lax.axis_size(axis)
        ends = count - 1
        head = lax.slice_in_dim(cells, 0, width, axis=dim)
        tail = lax.slice_in_dim(cells, cells.shape[dim] - width, cells.shape[dim], axis=dim)
        cells = jnp.concatenate(
            [
                lax.ppermute(tail, axis, [(i, (i + 1) % count) for i in range(ends)]),
                cells,
                lax.ppermute(head, axis, [((i + 1) % count, i) for i in range(ends)]),
            ],
            axis=dim,
        )
    return cells


def quadrant_table(side_cells, half_index):
    half_size = side_cells // 2
    row_ids = jnp.arange(side_cells, dtype=jnp.int32)[:, None]
    col_ids = jnp.arange(side_cells, dtype=jnp.int32)[None, :]
    base_cell = half_index * half_size
    near_cell = base_cell + row_ids // 2
    other_cell = near_cell + jnp.where(row_ids % 2 == 1, 1, -1)
    other_cell = jnp.clip(other_cell, base_cell, base_cell + half_size - 1)
    return 0.75 * (col_ids == near_cell).astype(jnp.float32) + 0.25 * (
        col_ids == other_cell
    ).astype(jnp.float32)


def refine_group(parents):
    side_cells = parents.shape[-1]
    tables = [quadrant_table(side_cells, 0), quadrant_table(side_cells, 1)]
    upper = [
        jnp.einsum("ij,njk->nik", table, parents, precision=lax.Precision.HIGHEST)
        for table in tables
    ]
    rows_out = []
    for half_x in range(2):
        pair = [
            jnp.einsum(
                "nik,lk->nil", upper[half_x], tables[half_y], precision=lax.Precision.HIGHEST
            )
            for half_y in range(2)
        ]
        rows_out.append(jnp.stack(pair, axis=1))
    return jnp.stack(rows_out, axis=1)


def spacing_factor(levels):
    return 1.0 + 3.0 * (levels >= 1).astype(jnp.float32)


def relax(field_pad, stretch_pad, bend_pad, load_core):
    center = field_pad[2:-2, 2:-2]
    laplace = (
        field_pad[:-2, 1:-1]
        + field_pad[2:, 1:-1]
        + field_pad[1:-1, :-2]
        + field_pad[1:-1, 2:]
        - 4.0 * field_pad[1:-1, 1:-1]
    )
    moment = bend_pad * laplace
    bending = (
        moment[:-2, 1:-1]
        + moment[2:, 1:-1]
        + moment[1:-1, :-2]
        + moment[1:-1, 2:]
        - 4.0 * moment[1:-1, 1:-1]
    )
    stretch_mid = stretch_pad[1:-1, 1:-1]
    diagonal = 16.0 * bend_pad[1:-1, 1:-1]
    stretching = jnp.zeros_like(center)
    neighbours = (
        (stretch_pad[:-2, 1:-1], bend_pad[:-2, 1:-1], field_pad[1:-3, 2:-2]),
        (stretch_pad[2:, 1:-1], bend_pad[2:, 1:-1], field_pad[3:-1, 2:-2]),
        (stretch_pad[1:-1, :-2], bend_pad[1:-1, :-2], field_pad[2:-2, 1:-3]),
        (stretch_pad[1:-1, 2:], bend_pad[1:-1, 2:], field_pad[2:-2, 3:-1]),
    )
    for near_stretch, near_bend, near_field in neighbours:
        face_coef = 0.5 * (stretch_mid + near_stretch)
        stretching = stretching + face_coef * (center - near_field)
        diagonal = diagonal + face_coef + near_bend
    remainder = load_core - (stretching + bending)
    return center + OMEGA * remainder / diagonal


def local(old_field, old_level, new_source, stretch_coef, bend_coef, load_field):
    per_device = old_field.shape[0]
    side_cells = old_field.shape[1]
    groups_x, groups_y = new_source.shape
    per_groups = groups_x * groups_y
    wide_count = lax.axis_size("wide")
    segments = lax.axis_size("narrow")
    my_rank = lax.axis_index("wide")
    capacity = max(2, per_groups // wide_count)
    route_table = lax.all_gather(new_source, "wide", axis=0, tiled=True)
    all_source = route_table.reshape(wide_count, per_groups)
    from_rank = all_source // per_device // segments
    from_local = all_source % per_device
    positions = jnp.arange(per_groups, dtype=jnp.int32)
    earlier = (positions[None, :] < positions[:, None]).astype(jnp.int32)
    same_rank = (from_rank[:, :, None] == from_rank[:, None, :]).astype(jnp.int32)
    slot_ids = jnp.sum(same_rank * earlier[None, :, :], axis=2)
    slot_range = jnp.arange(capacity, dtype=jnp.int32)
    chosen = (
        (from_rank[:, None, :] == my_rank) & (slot_ids[:, None, :] == slot_range[None, :, None])
    ).astype(jnp.int32)
    pick_local = jnp.sum(chosen * from_local[:, None, :], axis=2).reshape(-1)
    parents = old_field[pick_local]
    parent_spacing = spacing_factor(old_level[pick_local])
    own_index = from_rank[my_rank] * capacity + slot_ids[my_rank]
    arrived, arrived_spacing = (
        lax.all_to_all(
            parents.reshape(wide_count, capacity, side_cells, side_cells),
            "wide",
            split_axis=0,
            concat_axis=0,
            tiled=True,
        ),
        lax.all_to_all(
            parent_spacing.reshape(wide_count, capacity),
            "wide",
            split_axis=0,
            concat_axis=0,
            tiled=True,
        ),
    )
    blocks = refine_group(arrived.reshape(-1, side_cells, side_cells)[own_index])
    spacing = arrived_spacing.reshape(-1)[own_index]
    rows_here = groups_x * 2 * side_cells
    cols_here = groups_y * 2 * side_cells
    grid_field = (
        blocks.reshape(groups_x, groups_y, 2, 2, side_cells, side_cells)
        .transpose(0, 2, 4, 1, 3, 5)
        .reshape(rows_here, cols_here)
    )
    scale_grid = jnp.repeat(
        jnp.repeat(spacing.reshape(groups_x, groups_y), 2 * side_cells, axis=0),
        2 * side_cells,
        axis=1,
    )
    stretch_eff = stretch_coef * scale_grid
    bend_eff = bend_coef * scale_grid * scale_grid
    coeffs = padded_2(jnp.stack([stretch_eff, bend_eff]), (("wide", 1), ("narrow", 2)), 1)
    for sweep_index in range(SWEEPS):
        padded = padded_2(grid_field, (("wide", 0), ("narrow", 1)), 2)
        grid_field = relax(padded, coeffs[0], coeffs[1], load_field)
    return grid_field


def solution(mesh):
    return jax.shard_map(
        local,
        mesh=mesh,
        in_specs=(
            P(("wide", "narrow"), None, None),
            P(("wide", "narrow")),
            P("wide", "narrow"),
            P("wide", "narrow"),
            P("wide", "narrow"),
            P("wide", "narrow"),
        ),
        out_specs=P("wide", "narrow"),
        check_vma=False,
    )
```

profile of v0, /device:TPU:0, one launch (start us, length us, event | category | flops | bytes accessed | tf_op | source)
XLA Modules:
  0.0 180.0 jit_solution(6980610308925500247)
XLA Ops:
  0.0 10.6 %all-gather = s32[8,2,4]{2,1,0:T(2,128)S(1)} all-gather(s32[1,2,4]{2,1,0:T(2,128)} %bitcast.65), channel_id=1, replica_groups=mesh['wide'=8,'narrow'=4] {'wide'}, dimensions={0}, use_global_device_ids=true | all-gather | bytes 288 | tf_op jit(solution)/shard_map/all_gather | solution.py:108
  11.4 1.3 gather_fusion.2
  13.4 3.3 %all-to-all-start.1 = ((f32[8,1,2]{2,1,0:T(1,128)}), f32[8,1,2]{2,1,0:T(1,128)S(1)}, u32[]{:S(2)}, u32[]{:S(2)}) async-start(f32[8,1,2]{2,1,0:T(1,128)} %bitcast.16), calls=%async_computation.1 | async-start | bytes 8192 | tf_op jit(solution)/shard_map/all_to_all | solution.py:132
  16.8 1.6 gather_fusion
  18.4 2.9 %all-to-all-done.1 = f32[8,1,2]{2,1,0:T(1,128)S(1)} async-done(((f32[8,1,2]{2,1,0:T(1,128)}), f32[8,1,2]{2,1,0:T(1,128)S(1)}, u32[]{:S(2)}, u32[]{:S(2)}) %all-to-all-start.1) | async-done | bytes 96 | tf_op jit(solution)/shard_map/all_to_all | solution.py:132
  21.3 3.6 %all-to-all-start = ((f32[8,2,128,128]{3,2,1,0:T(8,128)}), f32[8,2,128,128]{3,2,1,0:T(8,128)S(1)}, u32[]{:S(2)}, u32[]{:S(2)}) async-start(f32[8,2,128,128]{3,2,1,0:T(8,128)} %bitcast.3), calls=%async_computation | async-start | bytes 2097152 | tf_op jit(solution)/shard_map/all_to_all | solution.py:125
  28.1 1.1 copy-done.15
  29.9 0.9 multiply_bitcast_fusion
  30.8 2.3 %collective-permute-start = (f32[2,1,1024]{2,1,0:T(1,128)S(1)}, f32[2,1,1024]{2,1,0:T(1,128)S(1)}, u32[]{:S(2)}, u32[]{:S(2)}) collective-permute-start(f32[2,1,1024]{2,1,0:T(1,128)S(1)} %get-tuple-element.11), channel_id=1, source_target_pairs={{0,4},{4,8},{8,12},{12,16},{16,20},{20,24},{24,28},{1,5},{5,9},{9,... | collective-permute-start | bytes 24584 | tf_op jit(solution)/shard_map/ppermute | solution.py:20
  33.1 1.5 collective-permute-start.1
  34.6 2.7 %collective-permute-done.1 = f32[2,1,1024]{2,1,0:T(1,128)S(1)} collective-permute-done((f32[2,1,1024]{2,1,0:T(1,128)S(1)}, f32[2,1,1024]{2,1,0:T(1,128)S(1)}, u32[]{:S(2)}, u32[]{:S(2)}) %collective-permute-start.1) | collective-permute-done | bytes 8224 | tf_op jit(solution)/shard_map/ppermute | solution.py:22
  37.3 2.8 %pad_maximum_fusion = f32[2,514,1024]{2,1,0:T(8,128)} fusion(f32[2,1,1024]{2,1,0:T(1,128)S(1)} %collective-permute-done.1, f32[1,512,1024]{2,1,0:T(8,128)S(1)} %get-tuple-element.24, f32[1,512,1024]{2,1,0:T(8,128)S(1)} %get-tuple-element.23, f32[2,1,1024]{2,1,0:T(1,128)S(1)} %collective-permute-done), kind=kLoop, calls=%fused_computation.4 | loop fusion | flops 3158016 | bytes 8421376 | tf_op jit(solution)/shard_map/concatenate | solution.py:18
  40.8 1.0 convolution_bitcast_fusion
  41.9 1.0 fusion.43
  42.9 1.0 convolution_bitcast_fusion.1
  44.0 1.0 fusion.48
  45.0 1.0 fusion.50
  46.1 1.0 fusion.46
  47.3 2.9 %copy.83 = f32[2,2,128,4,2,128]{5,4,3,2,1,0:T(2,128)} copy(f32[2,2,128,4,2,128]{5,2,3,0,4,1:T(8,128)S(1)} %maximum_bitcast_fusion) | data formatting | bytes 4194304 | tf_op jit(solution)/shard_map/transpose | solution.py:146
  50.2 2.9 %reshape.332 = f32[512,1024]{1,0:T(8,128)S(1)} reshape(f32[2,2,128,4,2,128]{5,4,3,2,1,0:T(2,128)} %copy.83) | data formatting | bytes 4194304 | tf_op jit(solution)/shard_map/reshape | solution.py:147
  53.2 4.5 %collective-permute-start.4 = (f32[2,1024]{1,0:T(2,128)S(1)}, f32[2,1024]{1,0:T(2,128)S(1)}, u32[]{:S(2)}, u32[]{:S(2)}) collective-permute-start(f32[2,1024]{1,0:T(2,128)S(1)} %get-tuple-element.25), channel_id=1, source_target_pairs={{0,4},{4,8},{8,12},{12,16},{16,20},{20,24},{24,28},{1,5},{5,9},{9,... | collective-permute-start | bytes 24584 | tf_op jit(solution)/shard_map/ppermute | solution.py:20
  57.7 1.3 collective-permute-start.5
  59.0 1.4 fusion.110
  60.7 1.3 collective-permute-start.3
  62.2 4.5 %collective-permute-start.2 = (f32[2,514,1]{1,0,2:T(2,128)S(1)}, f32[2,514,1]{1,0,2:T(2,128)S(1)}, u32[]{:S(2)}, u32[]{:S(2)}) collective-permute-start(f32[2,514,1]{1,0,2:T(2,128)S(1)} %copy.85), channel_id=1, source_target_pairs={{0,1},{1,2},{2,3},{4,5},{5,6},{6,7},{8,9},{9,10},{10,11},{12,13},{... | collective-permute-start | bytes 12344 | tf_op jit(solution)/shard_map/ppermute | solution.py:20
  67.0 1.1 collective-permute-done.2
  68.3 6.7 %concatenate.50 = f32[2,514,1026]{2,1,0:T(8,128)} concatenate(f32[2,514,1]{2,1,0:T(8,128)S(1)} %copy.87, f32[2,514,1024]{2,1,0:T(8,128)} %pad_maximum_fusion, f32[2,514,1]{2,1,0:T(8,128)S(1)} %copy.88), dimensions={2} | concatenate | bytes 8437824 | tf_op jit(solution)/shard_map/concatenate | solution.py:18
  75.2 1.3 copy-done.13
  76.7 1.4 collective-permute-start.7
  78.1 5.0 %collective-permute-start.6 = (f32[516,2]{1,0:T(8,128)S(1)}, f32[516,2]{1,0:T(8,128)S(1)}, u32[]{:S(2)}, u32[]{:S(2)}) collective-permute-start(f32[516,2]{1,0:T(8,128)S(1)} %get-tuple-element.16), channel_id=1, source_target_pairs={{0,1},{1,2},{2,3},{4,5},{5,6},{6,7},{8,9},{9,10},{10,11},{12,13},{... | collective-permute-start | bytes 12392 | tf_op jit(solution)/shard_map/ppermute | solution.py:20
  83.2 2.5 %slice_bitcast_fusion.1 = (f32[514,1026]{1,0:T(8,128)}, f32[514,1026]{1,0:T(8,128)}) fusion(f32[2,514,1026]{2,1,0:T(8,128)S(1)} %copy-done.4), kind=kLoop, calls=%fused_computation.19 | loop fusion | bytes 8437824 | tf_op jit(solution)/shard_map/squeeze | solution.py:159
  85.7 1.6 collective-permute-done.7
  87.3 1.2 collective-permute-done.6
  88.4 4.0 %concatenate.56 = f32[516,1028]{1,0:T(8,128)} concatenate(f32[516,2]{1,0:T(8,128)S(1)} %collective-permute-done.6, f32[516,1024]{1,0:T(8,128)} %copy-done.13, f32[516,2]{1,0:T(8,128)S(1)} %collective-permute-done.7), dimensions={1} | concatenate | bytes 4243584 | tf_op jit(solution)/shard_map/concatenate | solution.py:18
  94.1 6.3 %fusion.3 = f32[514,1026]{1,0:T(8,128)} fusion(f32[516,1028]{1,0:T(8,128)S(1)} %copy-done.6, f32[516,1026]{1,0:T(8,128)S(1)} %get-tuple-element.20, f32[516,1026]{1,0:T(8,128)S(1)} %get-tuple-element.19, f32[2,514,1026]{2,1,0:T(8,128)} %concatenate.50), kind=kLoop, calls=%fused_computation.14 | loop fusion | flops 3164184 | bytes 14766192 | tf_op jit(solution)/shard_map/mul | solution.py:74
  100.4 22.9 %fusion.29 = f32[512,1024]{1,0:T(8,128)S(1)} fusion(f32[512,1024]{1,0:T(8,128)} %copy-done.8, f32[512,1024]{1,0:T(8,128)} %param.11, f32[514,1026]{1,0:T(8,128)} %fusion.3, f32[516,1026]{1,0:T(8,128)} %copy-done.12, f32[516,1026]{1,0:T(8,128)} %copy-done.11, f32[2,1024]{1,0:T(2,128)S(1)} %collective-permute-done.5, f32[2,1024]{1,0:T(2,128)S(1)} %collective-permute-done.4, ...), kind=kLoop, calls=%fused_computation.65 | loop fusion | flops 20971520 | bytes 41959424 | tf_op jit(solution)/shard_map/add | solution.py:96
  123.3 1.3 collective-permute-start.8
  124.6 1.3 collective-permute-start.9
  125.9 4.1 %collective-permute-done.9 = f32[2,1024]{1,0:T(2,128)S(1)} collective-permute-done((f32[2,1024]{1,0:T(2,128)S(1)}, f32[2,1024]{1,0:T(2,128)S(1)}, u32[]{:S(2)}, u32[]{:S(2)}) %collective-permute-start.9) | collective-permute-done | bytes 8224 | tf_op jit(solution)/shard_map/ppermute | solution.py:22
  130.2 1.4 copy-done.14
  131.8 1.3 collective-permute-start.11
  133.1 5.3 %collective-permute-start.10 = (f32[516,2]{1,0:T(8,128)S(1)}, f32[516,2]{1,0:T(8,128)S(1)}, u32[]{:S(2)}, u32[]{:S(2)}) collective-permute-start(f32[516,2]{1,0:T(8,128)S(1)} %get-tuple-element.14), channel_id=1, source_target_pairs={{0,1},{1,2},{2,3},{4,5},{5,6},{6,7},{8,9},{9,10},{10,11},{12,13},{... | collective-permute-start | bytes 12392 | tf_op jit(solution)/shard_map/ppermute | solution.py:20
  138.4 3.3 %collective-permute-done.11 = f32[516,2]{1,0:T(8,128)S(1)} collective-permute-done((f32[516,2]{1,0:T(8,128)S(1)}, f32[516,2]{1,0:T(8,128)S(1)}, u32[]{:S(2)}, u32[]{:S(2)}) %collective-permute-start.11) | collective-permute-done | bytes 4160 | tf_op jit(solution)/shard_map/ppermute | solution.py:22
  141.6 1.7 collective-permute-done.10
  143.4 4.0 %concatenate.62 = f32[516,1028]{1,0:T(8,128)} concatenate(f32[516,2]{1,0:T(8,128)S(1)} %collective-permute-done.10, f32[516,1024]{1,0:T(8,128)} %copy-done.14, f32[516,2]{1,0:T(8,128)S(1)} %collective-permute-done.11), dimensions={1} | concatenate | bytes 4243584 | tf_op jit(solution)/shard_map/concatenate | solution.py:18
  148.3 1.4 copy-done.9
  150.4 5.5 %fusion.1 = f32[514,1026]{1,0:T(8,128)} fusion(f32[516,1028]{1,0:T(8,128)S(1)} %copy-done.5, f32[516,1026]{1,0:T(8,128)S(1)} %get-tuple-element.18, f32[516,1026]{1,0:T(8,128)S(1)} %get-tuple-element.17, f32[2,514,1026]{2,1,0:T(8,128)} %concatenate.50), kind=kLoop, calls=%fused_computation.8 | loop fusion | flops 3164184 | bytes 14766192 | tf_op jit(solution)/shard_map/mul | solution.py:74
  155.9 23.8 %fusion.10 = f32[512,1024]{1,0:T(8,128)} fusion(f32[512,1024]{1,0:T(8,128)} %copy-done.7, f32[512,1024]{1,0:T(8,128)} %param.11, f32[514,1026]{1,0:T(8,128)} %fusion.1, f32[516,1026]{1,0:T(8,128)} %copy-done.10, f32[516,1026]{1,0:T(8,128)} %copy-done.9, f32[2,1024]{1,0:T(2,128)S(1)} %collective-permute-done.9, f32[2,1024]{1,0:T(2,128)S(1)} %collective-permute-done.8, ...), kind=kLoop, calls=%fused_computation.33 | loop fusion | flops 20971520 | bytes 41959424 | tf_op jit(solution)/shard_map/add | solution.py:96
  (75 shorter events, 11.2 us)
Async XLA Ops:
  0.0 16.8 %copy-start = (f32[32,128,128]{2,1,0:T(8,128)S(1)}, f32[32,128,128]{2,1,0:T(8,128)}, u32[]{:S(2)}) copy-start(f32[32,128,128]{2,1,0:T(8,128)} %param.6) | copy-start | bytes 6291460
  13.4 7.9 %all-to-all-start.1 = ((f32[8,1,2]{2,1,0:T(1,128)}), f32[8,1,2]{2,1,0:T(1,128)S(1)}, u32[]{:S(2)}, u32[]{:S(2)}) async-start(f32[8,1,2]{2,1,0:T(1,128)} %bitcast.16), calls=%async_computation.1 | async-start | bytes 8192 | tf_op jit(solution)/shard_map/all_to_all | solution.py:132
  21.3 18.9 %all-to-all-start = ((f32[8,2,128,128]{3,2,1,0:T(8,128)}), f32[8,2,128,128]{3,2,1,0:T(8,128)S(1)}, u32[]{:S(2)}, u32[]{:S(2)}) async-start(f32[8,2,128,128]{3,2,1,0:T(8,128)} %bitcast.3), calls=%async_computation | async-start | bytes 2097152 | tf_op jit(solution)/shard_map/all_to_all | solution.py:125
  27.6 1.6 copy-start.15
  27.6 2.2 %copy-start.16 = (f32[512,1024]{1,0:T(8,128)S(1)}, f32[512,1024]{1,0:T(8,128)}, u32[]{:S(2)}) copy-start(f32[512,1024]{1,0:T(8,128)} %param.10) | copy-start | bytes 6291460
  30.8 3.8 %collective-permute-start = (f32[2,1,1024]{2,1,0:T(1,128)S(1)}, f32[2,1,1024]{2,1,0:T(1,128)S(1)}, u32[]{:S(2)}, u32[]{:S(2)}) collective-permute-start(f32[2,1,1024]{2,1,0:T(1,128)S(1)} %get-tuple-element.11), channel_id=1, source_target_pairs={{0,4},{4,8},{8,12},{12,16},{16,20},{20,24},{24,28},{1,5},{5,9},{9,... | collective-permute-start | bytes 24584 | tf_op jit(solution)/shard_map/ppermute | solution.py:20
  33.1 4.2 %collective-permute-start.1 = (f32[2,1,1024]{2,1,0:T(1,128)S(1)}, f32[2,1,1024]{2,1,0:T(1,128)S(1)}, u32[]{:S(2)}, u32[]{:S(2)}) collective-permute-start(f32[2,1,1024]{2,1,0:T(1,128)S(1)} %get-tuple-element.12), channel_id=1, source_target_pairs={{4,0},{8,4},{12,8},{16,12},{20,16},{24,20},{28,24},{5,1},{9,5},{13... | collective-permute-start | bytes 24584 | tf_op jit(solution)/shard_map/ppermute | solution.py:22
  53.2 39.3 %copy-start.8 = (f32[512,1024]{1,0:T(8,128)}, f32[512,1024]{1,0:T(8,128)S(1)}, u32[]{:S(2)}) copy-start(f32[512,1024]{1,0:T(8,128)S(1)} %reshape.332) | copy-start | bytes 6291460
  53.2 21.8 %collective-permute-start.4 = (f32[2,1024]{1,0:T(2,128)S(1)}, f32[2,1024]{1,0:T(2,128)S(1)}, u32[]{:S(2)}, u32[]{:S(2)}) collective-permute-start(f32[2,1024]{1,0:T(2,128)S(1)} %get-tuple-element.25), channel_id=1, source_target_pairs={{0,4},{4,8},{8,12},{12,16},{16,20},{20,24},{24,28},{1,5},{5,9},{9,... | collective-permute-start | bytes 24584 | tf_op jit(solution)/shard_map/ppermute | solution.py:20
  57.7 17.2 %collective-permute-start.5 = (f32[2,1024]{1,0:T(2,128)S(1)}, f32[2,1024]{1,0:T(2,128)S(1)}, u32[]{:S(2)}, u32[]{:S(2)}) collective-permute-start(f32[2,1024]{1,0:T(2,128)S(1)} %get-tuple-element.26), channel_id=1, source_target_pairs={{4,0},{8,4},{12,8},{16,12},{20,16},{24,20},{28,24},{5,1},{9,5},{13... | collective-permute-start | bytes 24584 | tf_op jit(solution)/shard_map/ppermute | solution.py:22
  60.7 6.1 %collective-permute-start.3 = (f32[2,514,1]{1,0,2:T(2,128)S(1)}, f32[2,514,1]{1,0,2:T(2,128)S(1)}, u32[]{:S(2)}, u32[]{:S(2)}) collective-permute-start(f32[2,514,1]{1,0,2:T(2,128)S(1)} %copy.86), channel_id=1, source_target_pairs={{1,0},{2,1},{3,2},{5,4},{6,5},{7,6},{9,8},{10,9},{11,10},{13,12},{... | collective-permute-start | bytes 12344 | tf_op jit(solution)/shard_map/ppermute | solution.py:22
  62.2 5.9 %collective-permute-start.2 = (f32[2,514,1]{1,0,2:T(2,128)S(1)}, f32[2,514,1]{1,0,2:T(2,128)S(1)}, u32[]{:S(2)}, u32[]{:S(2)}) collective-permute-start(f32[2,514,1]{1,0,2:T(2,128)S(1)} %copy.85), channel_id=1, source_target_pairs={{0,1},{1,2},{2,3},{4,5},{5,6},{6,7},{8,9},{9,10},{10,11},{12,13},{... | collective-permute-start | bytes 12344 | tf_op jit(solution)/shard_map/ppermute | solution.py:20
  74.9 8.2 %copy-start.4 = (f32[2,514,1026]{2,1,0:T(8,128)S(1)}, f32[2,514,1026]{2,1,0:T(8,128)}, u32[]{:S(2)}) copy-start(f32[2,514,1026]{2,1,0:T(8,128)} %concatenate.50) | copy-start | bytes 12656740
  75.2 1.3 copy-start.13
  76.7 10.6 %collective-permute-start.7 = (f32[516,2]{1,0:T(8,128)S(1)}, f32[516,2]{1,0:T(8,128)S(1)}, u32[]{:S(2)}, u32[]{:S(2)}) collective-permute-start(f32[516,2]{1,0:T(8,128)S(1)} %get-tuple-element.15), channel_id=1, source_target_pairs={{1,0},{2,1},{3,2},{5,4},{6,5},{7,6},{9,8},{10,9},{11,10},{13,12},{... | collective-permute-start | bytes 12392 | tf_op jit(solution)/shard_map/ppermute | solution.py:22
  78.1 10.3 %collective-permute-start.6 = (f32[516,2]{1,0:T(8,128)S(1)}, f32[516,2]{1,0:T(8,128)S(1)}, u32[]{:S(2)}, u32[]{:S(2)}) collective-permute-start(f32[516,2]{1,0:T(8,128)S(1)} %get-tuple-element.16), channel_id=1, source_target_pairs={{0,1},{1,2},{2,3},{4,5},{5,6},{6,7},{8,9},{9,10},{10,11},{12,13},{... | collective-permute-start | bytes 12392 | tf_op jit(solution)/shard_map/ppermute | solution.py:20
  92.5 1.7 copy-start.6
  93.3 7.1 %copy-start.11 = (f32[516,1026]{1,0:T(8,128)}, f32[516,1026]{1,0:T(8,128)S(1)}, u32[]{:S(2)}) copy-start(f32[516,1026]{1,0:T(8,128)S(1)} %get-tuple-element.19) | copy-start | bytes 6352996
  93.3 7.0 %copy-start.12 = (f32[516,1026]{1,0:T(8,128)}, f32[516,1026]{1,0:T(8,128)S(1)}, u32[]{:S(2)}) copy-start(f32[516,1026]{1,0:T(8,128)S(1)} %get-tuple-element.20) | copy-start | bytes 6352996
  94.1 6.3 %copy-start.2 = (f32[514,1026]{1,0:T(8,128)S(1)}, f32[514,1026]{1,0:T(8,128)}, u32[]{:S(2)}) copy-start(f32[514,1026]{1,0:T(8,128)} %get-tuple-element.7) | copy-start | bytes 6328372
  123.3 24.1 %copy-start.7 = (f32[512,1024]{1,0:T(8,128)}, f32[512,1024]{1,0:T(8,128)S(1)}, u32[]{:S(2)}) copy-start(f32[512,1024]{1,0:T(8,128)S(1)} %fusion.29) | copy-start | bytes 6291460
  123.3 2.6 %collective-permute-start.8 = (f32[2,1024]{1,0:T(2,128)S(1)}, f32[2,1024]{1,0:T(2,128)S(1)}, u32[]{:S(2)}, u32[]{:S(2)}) collective-permute-start(f32[2,1024]{1,0:T(2,128)S(1)} %get-tuple-element.21), channel_id=1, source_target_pairs={{0,4},{4,8},{8,12},{12,16},{16,20},{20,24},{24,28},{1,5},{5,9},{9,... | collective-permute-start | bytes 24584 | tf_op jit(solution)/shard_map/ppermute | solution.py:20
  124.6 5.4 %collective-permute-start.9 = (f32[2,1024]{1,0:T(2,128)S(1)}, f32[2,1024]{1,0:T(2,128)S(1)}, u32[]{:S(2)}, u32[]{:S(2)}) collective-permute-start(f32[2,1024]{1,0:T(2,128)S(1)} %get-tuple-element.22), channel_id=1, source_target_pairs={{4,0},{8,4},{12,8},{16,12},{20,16},{24,20},{28,24},{5,1},{9,5},{13... | collective-permute-start | bytes 24584 | tf_op jit(solution)/shard_map/ppermute | solution.py:22
  130.2 1.4 copy-start.14
  131.8 9.9 %collective-permute-start.11 = (f32[516,2]{1,0:T(8,128)S(1)}, f32[516,2]{1,0:T(8,128)S(1)}, u32[]{:S(2)}, u32[]{:S(2)}) collective-permute-start(f32[516,2]{1,0:T(8,128)S(1)} %get-tuple-element.13), channel_id=1, source_target_pairs={{1,0},{2,1},{3,2},{5,4},{6,5},{7,6},{9,8},{10,9},{11,10},{13,12},{... | collective-permute-start | bytes 12392 | tf_op jit(solution)/shard_map/ppermute | solution.py:22
  133.1 10.3 %collective-permute-start.10 = (f32[516,2]{1,0:T(8,128)S(1)}, f32[516,2]{1,0:T(8,128)S(1)}, u32[]{:S(2)}, u32[]{:S(2)}) collective-permute-start(f32[516,2]{1,0:T(8,128)S(1)} %get-tuple-element.14), channel_id=1, source_target_pairs={{0,1},{1,2},{2,3},{4,5},{5,6},{6,7},{8,9},{9,10},{10,11},{12,13},{... | collective-permute-start | bytes 12392 | tf_op jit(solution)/shard_map/ppermute | solution.py:20
  147.4 3.1 %copy-start.5 = (f32[516,1028]{1,0:T(8,128)S(1)}, f32[516,1028]{1,0:T(8,128)}, u32[]{:S(2)}) copy-start(f32[516,1028]{1,0:T(8,128)} %concatenate.62) | copy-start | bytes 6365380
  148.2 1.4 copy-start.9
  148.2 2.2 %copy-start.10 = (f32[516,1026]{1,0:T(8,128)}, f32[516,1026]{1,0:T(8,128)S(1)}, u32[]{:S(2)}) copy-start(f32[516,1026]{1,0:T(8,128)S(1)} %get-tuple-element.18) | copy-start | bytes 6352996
  150.4 5.5 %copy-start.3 = (f32[514,1026]{1,0:T(8,128)S(1)}, f32[514,1026]{1,0:T(8,128)}, u32[]{:S(2)}) copy-start(f32[514,1026]{1,0:T(8,128)} %get-tuple-element.7) | copy-start | bytes 6328372
  155.9 23.8 %copy-start.1 = (f32[32,128,128]{2,1,0:T(8,128)S(1)}, f32[32,128,128]{2,1,0:T(8,128)}, u32[]{:S(2)}) copy-start(f32[32,128,128]{2,1,0:T(8,128)} %param.6) | copy-start | bytes 6291460
where the time goes:
time: 183 us; the launch traced here: 180 us
  other arithmetic  65.8 us (36%)
  local copies, waits for them, and re-layouts  40 us (22%)
  starting transfers between devices  37.9 us (21%)
  waiting for transfers between devices  18.6 us (10%)
  blocking collectives  10.6 us (6%)
  matrix products  6.28 us (3%)
    add x2, other arithmetic, relax(): return center + OMEGA * remainder / diagonal  46.7 us
    ppermute x6, starting transfers between devices, padded_2(): lax.ppermute(tail, axis, [(i, (i + 1) % count) for i in range(ends)])  23 us
    concatenate x3, local copies, waits for them, and re-layouts, padded_2(): jnp.concatenate([lax.ppermute(tail, axis, [(i, (i + 1) % count) for i in...  14.7 us
    mul x2, other arithmetic, relax(): moment = bend_pad * laplace  11.8 us
    ppermute x6, waiting for transfers between devices, padded_2(): lax.ppermute(head, axis, [((i + 1) % count, i) for i in range(ends)])  11.6 us
    all_gather x1, blocking collectives, local(): route_table = lax.all_gather(new_source, 'wide', axis=0, tiled=True)  10.6 us
    ppermute x6, starting transfers between devices, padded_2(): lax.ppermute(head, axis, [((i + 1) % count, i) for i in range(ends)])  8.07 us
    unnamed x35, local copies, waits for them, and re-layouts  7.92 us
  transfers between devices with their start and end apart: 14, of which 9 were waited for; matrix products, arithmetic and copies ran while one was open for 11% of the time, Pallas kernels for 0%

commit v1 on v0

v1 whole, which is shorter than its diff:
```python
import functools

import jax
import jax.numpy as jnp
from jax import lax
from jax.experimental import pallas as pl
from jax.experimental.pallas import tpu as pltpu
from jax.sharding import PartitionSpec as P

SWEEPS = 2
OMEGA = 0.5
CAPACITY = 2
LANES = 128
EDGE = 16
HALO = 8
STEP = 16
SLOT = 8
PIECES = 4
MESH = pl.DeviceIdType.MESH


def refine_table(half, rows, cols):
    side = 2 * half
    base = jnp.where(rows >= side, half, 0)
    inner = jnp.where(rows >= side, rows - side, rows)
    near = base + (inner >> 1)
    other = near + jnp.where((inner & 1) == 1, 1, -1)
    other = jnp.minimum(jnp.maximum(other, base), base + half - 1)
    return jnp.where(cols == near, 0.75, 0.0) + jnp.where(cols == other, 0.25, 0.0)


def split3(x):
    high = x.astype(jnp.bfloat16)
    rest = x - high.astype(jnp.float32)
    mid = rest.astype(jnp.bfloat16)
    low = (rest - mid.astype(jnp.float32)).astype(jnp.bfloat16)
    return high, mid, low


def laplace(big):
    total, width = big.shape
    rows = total - 2 * HALO
    center = big[HALO : HALO + rows]
    above = pltpu.roll(big, 1, 0)[HALO : HALO + rows]
    below = pltpu.roll(big, total - 1, 0)[HALO : HALO + rows]
    left = pltpu.roll(center, 1, 1)
    right = pltpu.roll(center, width - 1, 1)
    return (above + below) + (left + right) - 4.0 * center, center


def kernel(
    wide_count, narrow_count, groups_x, groups_y,
    msg, old_hbm, stretch_hbm, bend_hbm, load_hbm, out_hbm,
    old, table, table_s, send, recv, grid, lap_u, weight, moment, rest, pack, unpacked, corner,
    table_row, table_col, result,
    load_sem, table_send, table_recv, smem_sem, par_send, par_recv, halo_send, halo_recv, out_sem,
):
    me = lax.axis_index("wide")
    seg = lax.axis_index("narrow")
    per_device, side, _ = old.shape
    per_groups = groups_x * groups_y
    span = 2 * side
    rows, cols = groups_x * span, groups_y * span
    width = cols + LANES
    chunk = rows * SLOT // LANES
    has_up, has_down = me > 0, me < wide_count - 1
    has_left, has_right = seg > 0, seg < narrow_count - 1
    up, down = lax.rem(me + wide_count - 1, wide_count), lax.rem(me + 1, wide_count)
    left, right = lax.rem(seg + narrow_count - 1, narrow_count), lax.rem(seg + 1, narrow_count)

    tile_rows = pl.ds(EDGE, rows)
    loads = [
        pltpu.make_async_copy(old_hbm, old, load_sem.at[0]),
        pltpu.make_async_copy(stretch_hbm, grid.at[0, tile_rows, pl.ds(0, cols)], load_sem.at[1]),
        pltpu.make_async_copy(bend_hbm, grid.at[1, tile_rows, pl.ds(0, cols)], load_sem.at[2]),
        pltpu.make_async_copy(load_hbm, grid.at[2, tile_rows, pl.ds(0, cols)], load_sem.at[3]),
    ]
    for copy in loads:
        copy.start()

    peers = [(lax.rem(me + k, wide_count), seg) for k in range(1, wide_count)]
    peers += [(me, left), (me, right), (up, left), (up, right), (down, left), (down, right)]
    barrier = pltpu.get_barrier_semaphore()
    for peer in peers:
        pl.semaphore_signal(barrier, inc=1, device_id=peer, device_id_type=MESH)
    pl.semaphore_wait(barrier, len(peers))

    table_copies = []
    for k in range(1, wide_count):
        copy = pltpu.make_async_remote_copy(
            src_ref=msg, dst_ref=table.at[me], send_sem=table_send.at[k], recv_sem=table_recv.at[k],
            device_id=(lax.rem(me + k, wide_count), seg), device_id_type=MESH,
        )
        copy.start()
        table_copies.append(copy)
    table[me] = msg[...]

    half = side // 2
    shape = (span, side)
    by_row = refine_table(
        half, lax.broadcasted_iota(jnp.int32, shape, 0), lax.broadcasted_iota(jnp.int32, shape, 1)
    ).astype(jnp.bfloat16)
    shape = (side, span)
    by_col = refine_table(
        half, lax.broadcasted_iota(jnp.int32, shape, 1), lax.broadcasted_iota(jnp.int32, shape, 0)
    ).astype(jnp.bfloat16)
    for part in range(3):
        table_row[:, part * side : (part + 1) * side] = by_row
        table_col[part * side : (part + 1) * side, :] = by_col

    for copy in table_copies:
        copy.wait()
    to_smem = pltpu.make_async_copy(table, table_s, smem_sem)
    to_smem.start()
    to_smem.wait()

    loads[0].wait()
    block = per_device * narrow_count

    def picks(dest):
        first, second, seen = jnp.int32(0), jnp.int32(0), jnp.int32(0)
        for j in range(per_groups):
            source = table_s[dest, 0, j]
            mine = lax.div(source, jnp.int32(block)) == me
            where = lax.rem(source, jnp.int32(per_device))
            first = jnp.where(mine & (seen == 0), where, first)
            second = jnp.where(mine & (seen == 1), where, second)
            seen = seen + mine.astype(jnp.int32)
        return first, second

    parent_copies = []
    for k in range(1, wide_count):
        dest = lax.rem(me + k, wide_count)
        first, second = picks(dest)
        send[k, 0] = old[first]
        send[k, 1] = old[second]
        copy = pltpu.make_async_remote_copy(
            src_ref=send.at[k], dst_ref=recv.at[me], send_sem=par_send.at[k], recv_sem=par_recv.at[k],
            device_id=(dest, seg), device_id_type=MESH,
        )
        copy.start()
        parent_copies.append(copy)
    first, second = picks(me)
    recv[me, 0] = old[first]
    recv[me, 1] = old[second]

    ranks = []
    places = []
    for j in range(per_groups):
        source = table_s[me, 0, j]
        rank = lax.div(source, jnp.int32(block))
        slot = jnp.int32(0)
        for earlier in ranks:
            slot = slot + (earlier == rank).astype(jnp.int32)
        ranks.append(rank)
        places.append((rank, jnp.minimum(slot, CAPACITY - 1)))
    loads[1].wait()
    loads[2].wait()
    loads[3].wait()
    for j in range(per_groups):
        source = table_s[me, 0, j]
        level = table_s[ranks[j], 0, per_groups + lax.rem(source, jnp.int32(per_device))]
        factor = jnp.where(level >= 1, 4.0, 1.0).astype(jnp.float32)
        at_row = EDGE + j // groups_y * span
        at_col = j % groups_y * span

        @pl.loop(0, span // 32)
        def _(i):
            here = pl.ds(pl.multiple_of(at_row + i * 32, 8), 32)
            there = pl.ds(at_col, span)
            grid[0, here, there] = grid[0, here, there] * (0.5 * factor)
            grid[1, here, there] = grid[1, here, there] * (factor * factor)

    lane = lax.broadcasted_iota(jnp.int32, (chunk, LANES), 1)

    def exchange(first_plane, planes, phase):
        picked = pl.ds(first_plane, planes)
        for plane in range(first_plane, first_plane + planes):
            to_left = jnp.zeros((chunk, LANES), jnp.float32)
            to_right = to_left
            for i in range(LANES // SLOT):
                here = pl.ds(EDGE + i * chunk, chunk)
                mine = (lane >= i * SLOT) & (lane < (i + 1) * SLOT)
                head = grid[plane, here, 0:LANES]
                tail = grid[plane, here, cols - LANES : cols]
                if i:
                    head = pltpu.roll(head, i * SLOT, 1)
                if (i + 1) * SLOT < LANES:
                    tail = pltpu.roll(tail, (i + 1) * SLOT, 1)
                to_left = jnp.where(mine, head, to_left)
                to_right = jnp.where(mine, tail, to_right)
            pack[0, plane] = to_left
            pack[1, plane] = to_right
        top, bottom = pl.ds(EDGE, HALO), pl.ds(EDGE + rows - HALO, HALO)
        over, under = pl.ds(EDGE - HALO, HALO), pl.ds(EDGE + rows, HALO)
        every = pl.ds(0, cols)
        first, last = pl.ds(0, LANES), pl.ds(cols - LANES, LANES)
        plan = [
            (grid.at[picked, top, every], grid.at[picked, under, every], (up, seg)),
            (grid.at[picked, bottom, every], grid.at[picked, over, every], (down, seg)),
            (pack.at[0, picked], unpacked.at[0, picked], (me, left)),
            (pack.at[1, picked], unpacked.at[1, picked], (me, right)),
            (grid.at[picked, top, first], corner.at[0, picked], (up, left)),
            (grid.at[picked, top, last], corner.at[1, picked], (up, right)),
            (grid.at[picked, bottom, first], corner.at[2, picked], (down, left)),
            (grid.at[picked, bottom, last], corner.at[3, picked], (down, right)),
        ]
        copies = []
        for i, (source, target, device) in enumerate(plan):
            copy = pltpu.make_async_remote_copy(
                src_ref=source, dst_ref=target,
                send_sem=halo_send.at[phase, i], recv_sem=halo_recv.at[phase, i],
                device_id=device, device_id_type=MESH,
            )
            copy.start()
            copies.append(copy)
        return copies

    edge_lane = lax.broadcasted_iota(jnp.int32, (HALO, LANES), 1)

    def settle(copies, first_plane, planes):
        for copy in copies:
            copy.wait()
        beside = pl.ds(cols, LANES)
        for plane in range(first_plane, first_plane + planes):
            from_right, from_left = unpacked[0, plane], unpacked[1, plane]
            inside = jnp.where(lane < LANES // 2, has_right.astype(jnp.int32), has_left.astype(jnp.int32)) > 0
            for i in range(LANES // SLOT):
                head, tail = from_right, from_left
                if i:
                    head = pltpu.roll(head, LANES - i * SLOT, 1)
                if (i + 1) * SLOT < LANES:
                    tail = pltpu.roll(tail, LANES - (i + 1) * SLOT, 1)
                joined = jnp.where(lane < LANES // 2, head, tail)
                grid[plane, pl.ds(EDGE + i * chunk, chunk), beside] = jnp.where(inside, joined, 0.0)
            for at, is_there, pair in ((EDGE + rows, has_down, 0), (EDGE - HALO, has_up, 2)):
                here = pl.ds(at, HALO)
                joined = jnp.where(edge_lane < LANES // 2, corner[pair, plane], corner[pair + 1, plane])
                keep = jnp.where(
                    edge_lane < LANES // 2, has_right.astype(jnp.int32), has_left.astype(jnp.int32)
                ) * is_there.astype(jnp.int32)
                grid[plane, here, beside] = jnp.where(keep > 0, joined, 0.0)
                every = grid[plane, here, 0:cols]
                grid[plane, here, 0:cols] = jnp.where(is_there, every, jnp.zeros_like(every))

    def clear_outside():
        beside = pl.ds(cols, LANES)
        total = rows + 2 * HALO
        inside_lane = lax.broadcasted_iota(jnp.int32, (total, LANES), 1)
        keep = jnp.where(inside_lane < LANES // 2, has_right.astype(jnp.int32), has_left.astype(jnp.int32)) > 0
        here = pl.ds(EDGE - HALO, total)
        grid[3, here, beside] = jnp.where(keep, grid[3, here, beside], 0.0)
        for at, is_there in ((EDGE + rows, has_down), (EDGE - HALO, has_up)):
            here = pl.ds(at, HALO)
            every = grid[3, here, :]
            grid[3, here, :] = jnp.where(is_there, every, jnp.zeros_like(every))

    steps = (rows + 2 * HALO) // STEP

    def window(i, start):
        at = start + i * STEP
        return pl.ds(pl.multiple_of(at - HALO, 8), STEP + 2 * HALO), pl.ds(pl.multiple_of(at, 8), STEP)

    settle(exchange(0, 3, 0), 0, 3)

    @pl.loop(0, steps)
    def _(i):
        around, here = window(i, EDGE - HALO)
        of_u, mid_u = laplace(grid[0, around, :])
        of_b, mid_b = laplace(grid[1, around, :])
        lap_u[here, :] = of_u
        weight[here, :] = OMEGA / (of_u + of_b + 8.0 * mid_u + 20.0 * mid_b)

    for copy in parent_copies:
        copy.wait()
    for j in range(per_groups):
        rank, slot = places[j]
        parent = recv[rank, slot]
        wider = jnp.dot(
            jnp.concatenate(split3(parent), axis=1), table_col[...], preferred_element_type=jnp.float32
        )
        child = jnp.dot(
            table_row[...], jnp.concatenate(split3(wider), axis=0), preferred_element_type=jnp.float32
        )
        grid[3, pl.ds(EDGE + j // groups_y * span, span), pl.ds(j % groups_y * span, span)] = child

    settle(exchange(3, 1, 1), 3, 1)

    def first_half():
        @pl.loop(0, steps)
        def _(i):
            around, here = window(i, EDGE - HALO)
            of_v, mid = laplace(grid[3, around, :])
            coef = grid[0, here, :]
            moment[here, :] = grid[1, here, :] * of_v - coef * mid
            rest[here, :] = grid[2, here, :] - (mid * lap_u[here, :] - coef * of_v)

    def second_half(i, start):
        around, here = window(i, start)
        of_m, _ = laplace(moment[around, :])
        return here, grid[3, here, :] + weight[here, :] * (rest[here, :] - of_m)

    for sweep in range(SWEEPS - 1):
        first_half()

        @pl.loop(0, steps)
        def _(i):
            here, value = second_half(i, EDGE - HALO)
            grid[3, here, :] = value

        clear_outside()

    first_half()
    piece = rows // PIECES
    stores = []
    for p in range(PIECES):

        @pl.loop(0, piece // STEP)
        def _(i):
            _, value = second_half(i, EDGE + p * piece)
            result[pl.ds(pl.multiple_of(p * piece + i * STEP, 8), STEP), :] = value[:, 0:cols]

        part = pl.ds(p * piece, piece)
        copy = pltpu.make_async_copy(result.at[part, :], out_hbm.at[part, :], out_sem.at[p])
        copy.start()
        stores.append(copy)
    for copy in stores:
        copy.wait()


def local(old_field, old_level, new_source, stretch_coef, bend_coef, load_field):
    wide_count = lax.axis_size("wide")
    narrow_count = lax.axis_size("narrow")
    groups_x, groups_y = new_source.shape
    per_device, side, _ = old_field.shape
    rows, cols = stretch_coef.shape
    used = groups_x * groups_y + per_device
    length = -(-used // LANES) * LANES
    msg = jnp.concatenate(
        [new_source.reshape(-1), old_level, jnp.zeros((length - used,), jnp.int32)]
    ).reshape(1, length)
    full = (rows + 2 * EDGE, cols + LANES)
    chunk = rows * SLOT // LANES
    span = 2 * side
    f32 = jnp.float32
    dma = pltpu.SemaphoreType.DMA
    return pl.pallas_call(
        functools.partial(kernel, wide_count, narrow_count, groups_x, groups_y),
        out_shape=jax.ShapeDtypeStruct((rows, cols), f32),
        in_specs=[pl.BlockSpec(memory_space=pltpu.VMEM)] + [pl.BlockSpec(memory_space=pl.ANY)] * 4,
        out_specs=pl.BlockSpec(memory_space=pl.ANY),
        scratch_shapes=[
            pltpu.VMEM(old_field.shape, f32),
            pltpu.VMEM((wide_count, 1, length), jnp.int32),
            pltpu.SMEM((wide_count, 1, length), jnp.int32),
            pltpu.VMEM((wide_count, CAPACITY, side, side), f32),
            pltpu.VMEM((wide_count, CAPACITY, side, side), f32),
            pltpu.VMEM((4,) + full, f32),
            pltpu.VMEM(full, f32),
            pltpu.VMEM(full, f32),
            pltpu.VMEM(full, f32),
            pltpu.VMEM(full, f32),
            pltpu.VMEM((2, 4, chunk, LANES), f32),
            pltpu.VMEM((2, 4, chunk, LANES), f32),
            pltpu.VMEM((4, 4, HALO, LANES), f32),
            pltpu.VMEM((span, 3 * side), jnp.bfloat16),
            pltpu.VMEM((3 * side, span), jnp.bfloat16),
            pltpu.VMEM((rows, cols), f32),
            dma((4,)),
            dma((wide_count,)),
            dma((wide_count,)),
            dma,
            dma((wide_count,)),
            dma((wide_count,)),
            dma((2, 8)),
            dma((2, 8)),
            dma((PIECES,)),
        ],
        compiler_params=pltpu.CompilerParams(
            collective_id=0, has_side_effects=True, vmem_limit_bytes=52 * 1024 * 1024
        ),
    )(msg, old_field, stretch_coef, bend_coef, load_field)


def solution(mesh):
    return jax.shard_map(
        local,
        mesh=mesh,
        in_specs=(
            P(("wide", "narrow"), None, None),
            P(("wide", "narrow")),
            P("wide", "narrow"),
            P("wide", "narrow"),
            P("wide", "narrow"),
            P("wide", "narrow"),
        ),
        out_specs=P("wide", "narrow"),
        check_vma=False,
    )
```

time: 183 us -> 58.9 us (0.32); the launches traced: 180 us -> 58.7 us
  other arithmetic: 65.8 us -> 0.73 us
  Pallas kernels: 0 us -> 54.1 us
  starting transfers between devices: 37.9 us -> 0 us
  local copies, waits for them, and re-layouts: 40 us -> 3.92 us
  waiting for transfers between devices: 18.6 us -> 0 us
  blocking collectives: 10.6 us -> 0 us
  matrix products: 6.28 us -> 0 us
    pallas_call x0 -> x1, Pallas kernels: none -> 54.1 us  [local(): pl.pallas_call(functools.partial(kernel, wide_count, narrow_count, groups...]
    add x3 -> x0, other arithmetic: 46.7 us -> none  [the longest x2 46.7 us: relax(): return center + OMEGA * remainder / diagonal]
    ppermute x12 -> x0, starting transfers between devices: 31.1 us -> none  [the longest x6 23 us: padded_2(): lax.ppermute(tail, axis, [(i, (i + 1) % count) for i in range(ends)])]
    ppermute x12 -> x0, waiting for transfers between devices: 15.6 us -> none  [the longest x6 11.6 us: padded_2(): lax.ppermute(head, axis, [((i + 1) % count, i) for i in range(ends)])]
    concatenate x3 -> x0, local copies, waits for them, and re-layouts: 14.7 us -> none  [padded_2(): jnp.concatenate([lax.ppermute(tail, axis, [(i, (i + 1) % count) for i in...]
    mul x2 -> x0, other arithmetic: 11.8 us -> none  [relax(): moment = bend_pad * laplace]
    all_gather x1 -> x0, blocking collectives: 10.6 us -> none  [local(): route_table = lax.all_gather(new_source, 'wide', axis=0, tiled=True)]
    all_to_all x2 -> x0, starting transfers between devices: 6.87 us -> none  [the longest x1 3.56 us: local(): lax.all_to_all(parents.reshape(wide_count, capacity, side_cells, side_cel...]
  transfers between devices with their start and end apart: 14 -> 0, of which waited for: 9 -> 0; matrix products, arithmetic and copies ran while one was open for 11% -> 0% of each run, Pallas kernels for 0% -> 0%
where the time goes in v1:
time: 58.9 us; the launch traced here: 58.7 us
  Pallas kernels  54.1 us (92%)
  local copies, waits for them, and re-layouts  3.92 us (7%)
  other arithmetic  0.73 us (1%)
    pallas_call x1, Pallas kernels, local(): pl.pallas_call(functools.partial(kernel, wide_count, narrow_count, groups...  54.1 us
    unnamed x1, local copies, waits for them, and re-layouts  3.16 us

profile of v1, /device:TPU:0, one launch (start us, length us, event | category | flops | bytes accessed | tf_op | source)
XLA Modules:
  0.0 58.7 jit_solution(6215667853515724104)
XLA Ops:
  0.0 0.8 %reshape.6 = s32[8]{0:T(128)S(1)} reshape(s32[2,4]{1,0:T(2,128)} %param.8) | data formatting | bytes 64 | tf_op jit(solution)/shard_map/reshape | solution.py:340
  0.8 0.7 %add_bitcast_fusion.msg = s32[1,128]{1,0:T(1,128)S(1)} fusion(s32[88]{0:T(128)S(1)} %broadcast_in_dim.3, s32[32]{0:T(128)} %param.7, s32[8]{0:T(128)S(1)} %reshape.6), kind=kLoop, calls=%fused_computation | loop fusion | flops 256 | bytes 1024 | tf_op jit(solution)/shard_map/reshape | solution.py:341
  1.5 54.1 %shard_map.64 = f32[512,1024]{1,0:T(8,128)} custom-call(s32[1,128]{1,0:T(1,128)S(1)} %add_bitcast_fusion.msg, f32[32,128,128]{2,1,0:T(8,128)} %old_hbm.1, f32[512,1024]{1,0:T(8,128)} %stretch_hbm.1, f32[512,1024]{1,0:T(8,128)} %bend_hbm.1, f32[512,1024]{1,0:T(8,128)} %load_hbm.1), custom_call_target="tpu_custom_call" | custom-call | tf_op jit(solution)/shard_map/pallas_call | solution.py:347
  55.6 3.2 %copy.8 = f32[512,1024]{1,0:T(8,128)} copy(f32[512,1024]{1,0:T(8,128)} %shard_map.64) | data formatting | bytes 4194304
  (1 shorter events, 0.0 us)

commit v2 on v1

--- a/solution.py
+++ b/solution.py
@@ -13,7 +13,6 @@
 LANES = 128
 EDGE = 16
 HALO = 8
-STEP = 16
 SLOT = 8
 PIECES = 4
 MESH = pl.DeviceIdType.MESH
@@ -37,22 +36,42 @@
     return high, mid, low
 
 
-def laplace(big):
-    total, width = big.shape
-    rows = total - 2 * HALO
-    center = big[HALO : HALO + rows]
-    above = pltpu.roll(big, 1, 0)[HALO : HALO + rows]
-    below = pltpu.roll(big, total - 1, 0)[HALO : HALO + rows]
-    left = pltpu.roll(center, 1, 1)
-    right = pltpu.roll(center, width - 1, 1)
-    return (above + below) + (left + right) - 4.0 * center, center
+def step_of(total):
+    return max(k for k in range(8, 65, 8) if total % k == 0)
+
+
+def laplace(load, count, tiles, ring):
+    lane = lax.broadcasted_iota(jnp.int32, (count, LANES), 1)
+    kept = {}
+
+    def tile(i):
+        if i not in kept:
+            kept[i] = {"big": load(i)}
+        return kept[i]
+
+    def turned(i, shift):
+        held = tile(i)
+        if shift not in held:
+            held[shift] = pltpu.roll(held["big"][HALO : HALO + count], shift, 1)
+        return held[shift]
+
+    for i in tiles:
+        big = tile(i)["big"]
+        center = big[HALO : HALO + count]
+        above = pltpu.roll(big, 1, 0)[HALO : HALO + count]
+        below = pltpu.roll(big, count + 2 * HALO - 1, 0)[HALO : HALO + count]
+        left = jnp.where(lane == 0, turned((i - 1) % ring, 1), turned(i, 1))
+        right = jnp.where(
+            lane == LANES - 1, turned((i + 1) % ring, LANES - 1), turned(i, LANES - 1)
+        )
+        yield i, (above + below) + (left + right) - 4.0 * center, center
 
 
 def kernel(
     wide_count, narrow_count, groups_x, groups_y,
-    msg, old_hbm, stretch_hbm, bend_hbm, load_hbm, out_hbm,
+    source_s, level_s, old_hbm, stretch_hbm, bend_hbm, load_hbm, out_hbm,
     old, table, table_s, send, recv, grid, lap_u, weight, moment, rest, pack, unpacked, corner,
-    table_row, table_col, result,
+    table_row, table_col, result, msg,
     load_sem, table_send, table_recv, smem_sem, par_send, par_recv, halo_send, halo_recv, out_sem,
 ):
     me = lax.axis_index("wide")
@@ -77,6 +96,14 @@
     ]
     for copy in loads:
         copy.start()
+
+    at_lane = lax.broadcasted_iota(jnp.int32, msg.shape, 1)
+    words = jnp.zeros(msg.shape, jnp.int32)
+    for j in range(per_groups):
+        words = jnp.where(at_lane == j, source_s[j // groups_y, j % groups_y], words)
+    for j in range(per_device):
+        words = jnp.where(at_lane == per_groups + j, level_s[j], words)
+    msg[...] = words
 
     peers = [(lax.rem(me + k, wide_count), seg) for k in range(1, wide_count)]
     peers += [(me, left), (me, right), (up, left), (up, right), (down, left), (down, right)]
@@ -255,21 +282,33 @@
             every = grid[3, here, :]
             grid[3, here, :] = jnp.where(is_there, every, jnp.zeros_like(every))
 
-    steps = (rows + 2 * HALO) // STEP
-
-    def window(i, start):
-        at = start + i * STEP
-        return pl.ds(pl.multiple_of(at - HALO, 8), STEP + 2 * HALO), pl.ds(pl.multiple_of(at, 8), STEP)
+    ring = width // LANES
+    whole = list(range(ring))
+
+    def sweep_rows(body, start, total):
+        step = step_of(total)
+
+        def one(at):
+            around = pl.ds(pl.multiple_of(at - HALO, 8), step + 2 * HALO)
+            body(around, pl.ds(pl.multiple_of(at, 8), step), at, step)
+
+        if total == step:
+            one(start)
+        else:
+            pl.loop(0, total // step)(lambda i: one(start + i * step))
+
+    def lanes(i):
+        return pl.ds(i * LANES, LANES)
+
+    def coefficients(around, here, at, step):
+        of_u = laplace(lambda i: grid[0, around, lanes(i)], step, whole, ring)
+        of_b = laplace(lambda i: grid[1, around, lanes(i)], step, whole, ring)
+        for (i, lap_a, mid_u), (_, lap_b, mid_b) in zip(of_u, of_b):
+            lap_u[here, lanes(i)] = lap_a
+            weight[here, lanes(i)] = OMEGA / (lap_a + lap_b + 8.0 * mid_u + 20.0 * mid_b)
 
     settle(exchange(0, 3, 0), 0, 3)
-
-    @pl.loop(0, steps)
-    def _(i):
-        around, here = window(i, EDGE - HALO)
-        of_u, mid_u = laplace(grid[0, around, :])
-        of_b, mid_b = laplace(grid[1, around, :])
-        lap_u[here, :] = of_u
-        weight[here, :] = OMEGA / (of_u + of_b + 8.0 * mid_u + 20.0 * mid_b)
+    sweep_rows(coefficients, EDGE - HALO, rows + 2 * HALO)
 
     for copy in parent_copies:
         copy.wait()
@@ -284,42 +323,51 @@
         )
         grid[3, pl.ds(EDGE + j // groups_y * span, span), pl.ds(j % groups_y * span, span)] = child
 
-    settle(exchange(3, 1, 1), 3, 1)
-
-    def first_half():
-        @pl.loop(0, steps)
-        def _(i):
-            around, here = window(i, EDGE - HALO)
-            of_v, mid = laplace(grid[3, around, :])
-            coef = grid[0, here, :]
-            moment[here, :] = grid[1, here, :] * of_v - coef * mid
-            rest[here, :] = grid[2, here, :] - (mid * lap_u[here, :] - coef * of_v)
-
-    def second_half(i, start):
-        around, here = window(i, start)
-        of_m, _ = laplace(moment[around, :])
-        return here, grid[3, here, :] + weight[here, :] * (rest[here, :] - of_m)
-
-    for sweep in range(SWEEPS - 1):
-        first_half()
-
-        @pl.loop(0, steps)
-        def _(i):
-            here, value = second_half(i, EDGE - HALO)
-            grid[3, here, :] = value
-
-        clear_outside()
-
-    first_half()
+    def first_half(tiles, start, total):
+        def body(around, here, at, step):
+            for i, of_v, mid in laplace(lambda i: grid[3, around, lanes(i)], step, tiles, ring):
+                coef = grid[0, here, lanes(i)]
+                moment[here, lanes(i)] = grid[1, here, lanes(i)] * of_v - coef * mid
+                rest[here, lanes(i)] = grid[2, here, lanes(i)] - (
+                    mid * lap_u[here, lanes(i)] - coef * of_v
+                )
+
+        sweep_rows(body, start, total)
+
+    def second_half(tiles, start, total, store):
+        def body(around, here, at, step):
+            for i, of_m, _ in laplace(lambda i: moment[around, lanes(i)], step, tiles, ring):
+                store(
+                    at, step, here, i,
+                    grid[3, here, lanes(i)] + weight[here, lanes(i)] * (rest[here, lanes(i)] - of_m),
+                )
+
+        sweep_rows(body, start, total)
+
+    strip = EDGE + HALO
+    copies = exchange(3, 1, 1)
+    first_half(whole[1:-2], 2 * EDGE, rows - 2 * EDGE)
+    settle(copies, 3, 1)
+    first_half(whole[-2:] + whole[:1], 2 * EDGE, rows - 2 * EDGE)
+    first_half(whole, EDGE - HALO, strip)
+    first_half(whole, rows, strip)
+
+    def keep_field(at, step, here, i, value):
+        grid[3, here, lanes(i)] = value
+
+    def keep_result(at, step, here, i, value):
+        result[pl.ds(pl.multiple_of(at - EDGE, 8), step), lanes(i)] = value
+
+    for sweep in range(SWEEPS):
+        if sweep:
+            first_half(whole, EDGE - HALO, rows + 2 * HALO)
+        if sweep < SWEEPS - 1:
+            second_half(whole, EDGE - HALO, rows + 2 * HALO, keep_field)
+            clear_outside()
     piece = rows // PIECES
     stores = []
     for p in range(PIECES):
-
-        @pl.loop(0, piece // STEP)
-        def _(i):
-            _, value = second_half(i, EDGE + p * piece)
-            result[pl.ds(pl.multiple_of(p * piece + i * STEP, 8), STEP), :] = value[:, 0:cols]
-
+        second_half(whole[:-1], EDGE + p * piece, piece, keep_result)
         part = pl.ds(p * piece, piece)
         copy = pltpu.make_async_copy(result.at[part, :], out_hbm.at[part, :], out_sem.at[p])
         copy.start()
@@ -336,9 +384,6 @@
     rows, cols = stretch_coef.shape
     used = groups_x * groups_y + per_device
     length = -(-used // LANES) * LANES
-    msg = jnp.concatenate(
-        [new_source.reshape(-1), old_level, jnp.zeros((length - used,), jnp.int32)]
-    ).reshape(1, length)
     full = (rows + 2 * EDGE, cols + LANES)
     chunk = rows * SLOT // LANES
     span = 2 * side
@@ -347,7 +392,7 @@
     return pl.pallas_call(
         functools.partial(kernel, wide_count, narrow_count, groups_x, groups_y),
         out_shape=jax.ShapeDtypeStruct((rows, cols), f32),
-        in_specs=[pl.BlockSpec(memory_space=pltpu.VMEM)] + [pl.BlockSpec(memory_space=pl.ANY)] * 4,
+        in_specs=[pl.BlockSpec(memory_space=pltpu.SMEM)] * 2 + [pl.BlockSpec(memory_space=pl.ANY)] * 4,
         out_specs=pl.BlockSpec(memory_space=pl.ANY),
         scratch_shapes=[
             pltpu.VMEM(old_field.shape, f32),
@@ -366,6 +411,7 @@
             pltpu.VMEM((span, 3 * side), jnp.bfloat16),
             pltpu.VMEM((3 * side, span), jnp.bfloat16),
             pltpu.VMEM((rows, cols), f32),
+            pltpu.VMEM((1, length), jnp.int32),
             dma((4,)),
             dma((wide_count,)),
             dma((wide_count,)),
@@ -379,7 +425,7 @@
         compiler_params=pltpu.CompilerParams(
             collective_id=0, has_side_effects=True, vmem_limit_bytes=52 * 1024 * 1024
         ),
-    )(msg, old_field, stretch_coef, bend_coef, load_field)
+    )(new_source, old_level, old_field, stretch_coef, bend_coef, load_field)
 
 
 def solution(mesh):

time: 58.9 us -> 50 us (0.85)
  Pallas kernels: 54.1 us -> 45.3 us
  other arithmetic: 0.73 us -> 0 us
    pallas_call x1, Pallas kernels: 54.1 us -> 45.3 us  [local(): pl.pallas_call(functools.partial(kernel, wide_count, narrow_count, groups...]
    unnamed x1 -> x5, local copies, waits for them, and re-layouts: 3.16 us -> 4.49 us
    reshape x1 -> x0, local copies, waits for them, and re-layouts: 0.76 us -> none  [local(): new_source.reshape(-1)]
    reshape x1 -> x0, other arithmetic: 0.73 us -> none  [local(): msg = jnp.concatenate([new_source.reshape(-1), old_level, jnp.zeros((leng...]
where the time goes in v2:
time: 50 us; the launch traced here: 49.8 us
  Pallas kernels  45.3 us (91%)
  local copies, waits for them, and re-layouts  4.49 us (9%)
    pallas_call x1, Pallas kernels, local(): pl.pallas_call(functools.partial(kernel, wide_count, narrow_count, groups...  45.3 us
    unnamed x5, local copies, waits for them, and re-layouts  4.49 us

profile of v2, /device:TPU:0, one launch (start us, length us, event | category | flops | bytes accessed | tf_op | source)
XLA Modules:
  0.0 49.8 jit_solution(5525638211831967359)
XLA Ops:
  0.0 0.0 copy-start
  0.0 0.7 %copy-done = s32[2,4]{1,0:T(2,128)S(1)} copy-done((s32[2,4]{1,0:T(2,128)S(1)}, s32[2,4]{1,0:T(2,128)}, u32[]{:S(2)}) %copy-start) | copy-done | bytes 56
  0.7 0.0 copy-start.1
  0.7 0.7 %copy-done.1 = s32[32]{0:T(128)S(1)} copy-done((s32[32]{0:T(128)S(1)}, s32[32]{0:T(128)}, u32[]{:S(2)}) %copy-start.1) | copy-done | bytes 152
  1.3 45.3 %shard_map.64 = f32[512,1024]{1,0:T(8,128)} custom-call(s32[2,4]{1,0:T(2,128)S(1)} %copy-done, s32[32]{0:T(128)S(1)} %copy-done.1, f32[32,128,128]{2,1,0:T(8,128)} %old_hbm.1, f32[512,1024]{1,0:T(8,128)} %stretch_hbm.1, f32[512,1024]{1,0:T(8,128)} %bend_hbm.1, f32[512,1024]{1,0:T(8,128)} %load_hbm.1), custom_call_target="tpu_custom_call" | custom-call | tf_op jit(solution)/shard_map/pallas_call | solution.py:392
  46.6 3.2 %copy.8 = f32[512,1024]{1,0:T(8,128)} copy(f32[512,1024]{1,0:T(8,128)} %shard_map.64) | data formatting | bytes 4194304
Async XLA Ops:
  0.0 0.7 %copy-start = (s32[2,4]{1,0:T(2,128)S(1)}, s32[2,4]{1,0:T(2,128)}, u32[]{:S(2)}) copy-start(s32[2,4]{1,0:T(2,128)} %source_s.1) | copy-start | bytes 100
  0.7 0.7 %copy-start.1 = (s32[32]{0:T(128)S(1)}, s32[32]{0:T(128)}, u32[]{:S(2)}) copy-start(s32[32]{0:T(128)} %level_s.1) | copy-start | bytes 388

commit v3 on v2

--- a/solution.py
+++ b/solution.py
@@ -46,20 +46,17 @@
 
     def tile(i):
         if i not in kept:
-            kept[i] = {"big": load(i)}
+            kept[i] = {"center": load(i, 0)}
         return kept[i]
 
     def turned(i, shift):
         held = tile(i)
         if shift not in held:
-            held[shift] = pltpu.roll(held["big"][HALO : HALO + count], shift, 1)
+            held[shift] = pltpu.roll(held["center"], shift, 1)
         return held[shift]
 
     for i in tiles:
-        big = tile(i)["big"]
-        center = big[HALO : HALO + count]
-        above = pltpu.roll(big, 1, 0)[HALO : HALO + count]
-        below = pltpu.roll(big, count + 2 * HALO - 1, 0)[HALO : HALO + count]
+        center, above, below = tile(i)["center"], load(i, -1), load(i, 1)
         left = jnp.where(lane == 0, turned((i - 1) % ring, 1), turned(i, 1))
         right = jnp.where(
             lane == LANES - 1, turned((i + 1) % ring, LANES - 1), turned(i, LANES - 1)
@@ -80,7 +77,6 @@
     per_groups = groups_x * groups_y
     span = 2 * side
     rows, cols = groups_x * span, groups_y * span
-    width = cols + LANES
     chunk = rows * SLOT // LANES
     has_up, has_down = me > 0, me < wide_count - 1
     has_left, has_right = seg > 0, seg < narrow_count - 1
@@ -88,12 +84,18 @@
     left, right = lax.rem(seg + narrow_count - 1, narrow_count), lax.rem(seg + 1, narrow_count)
 
     tile_rows = pl.ds(EDGE, rows)
-    loads = [
-        pltpu.make_async_copy(old_hbm, old, load_sem.at[0]),
-        pltpu.make_async_copy(stretch_hbm, grid.at[0, tile_rows, pl.ds(0, cols)], load_sem.at[1]),
-        pltpu.make_async_copy(bend_hbm, grid.at[1, tile_rows, pl.ds(0, cols)], load_sem.at[2]),
-        pltpu.make_async_copy(load_hbm, grid.at[2, tile_rows, pl.ds(0, cols)], load_sem.at[3]),
-    ]
+    tiles = cols // LANES
+    ring = tiles + 1
+    loads = [pltpu.make_async_copy(old_hbm, old, load_sem.at[0])]
+    for plane, source in enumerate((stretch_hbm, bend_hbm, load_hbm)):
+        for i in range(tiles):
+            loads.append(
+                pltpu.make_async_copy(
+                    source.at[:, pl.ds(i * LANES, LANES)],
+                    grid.at[plane, i, tile_rows, :],
+                    load_sem.at[1 + plane * tiles + i],
+                )
+            )
     for copy in loads:
         copy.start()
 
@@ -181,9 +183,8 @@
             slot = slot + (earlier == rank).astype(jnp.int32)
         ranks.append(rank)
         places.append((rank, jnp.minimum(slot, CAPACITY - 1)))
-    loads[1].wait()
-    loads[2].wait()
-    loads[3].wait()
+    for copy in loads[1:]:
+        copy.wait()
     for j in range(per_groups):
         source = table_s[me, 0, j]
         level = table_s[ranks[j], 0, per_groups + lax.rem(source, jnp.int32(per_device))]
@@ -194,9 +195,9 @@
         @pl.loop(0, span // 32)
         def _(i):
             here = pl.ds(pl.multiple_of(at_row + i * 32, 8), 32)
-            there = pl.ds(at_col, span)
-            grid[0, here, there] = grid[0, here, there] * (0.5 * factor)
-            grid[1, here, there] = grid[1, here, there] * (factor * factor)
+            for t in range(at_col // LANES, (at_col + span) // LANES):
+                grid[0, t, here, :] = grid[0, t, here, :] * (0.5 * factor)
+                grid[1, t, here, :] = grid[1, t, here, :] * (factor * factor)
 
     lane = lax.broadcasted_iota(jnp.int32, (chunk, LANES), 1)
 
@@ -208,8 +209,8 @@
             for i in range(LANES // SLOT):
                 here = pl.ds(EDGE + i * chunk, chunk)
                 mine = (lane >= i * SLOT) & (lane < (i + 1) * SLOT)
-                head = grid[plane, here, 0:LANES]
-                tail = grid[plane, here, cols - LANES : cols]
+                head = grid[plane, 0, here, :]
+                tail = grid[plane, tiles - 1, here, :]
                 if i:
                     head = pltpu.roll(head, i * SLOT, 1)
                 if (i + 1) * SLOT < LANES:
@@ -220,17 +221,17 @@
             pack[1, plane] = to_right
         top, bottom = pl.ds(EDGE, HALO), pl.ds(EDGE + rows - HALO, HALO)
         over, under = pl.ds(EDGE - HALO, HALO), pl.ds(EDGE + rows, HALO)
-        every = pl.ds(0, cols)
-        first, last = pl.ds(0, LANES), pl.ds(cols - LANES, LANES)
+        every = pl.ds(0, tiles)
+        first, last = 0, tiles - 1
         plan = [
-            (grid.at[picked, top, every], grid.at[picked, under, every], (up, seg)),
-            (grid.at[picked, bottom, every], grid.at[picked, over, every], (down, seg)),
+            (grid.at[picked, every, top, :], grid.at[picked, every, under, :], (up, seg)),
+            (grid.at[picked, every, bottom, :], grid.at[picked, every, over, :], (down, seg)),
             (pack.at[0, picked], unpacked.at[0, picked], (me, left)),
             (pack.at[1, picked], unpacked.at[1, picked], (me, right)),
-            (grid.at[picked, top, first], corner.at[0, picked], (up, left)),
-            (grid.at[picked, top, last], corner.at[1, picked], (up, right)),
-            (grid.at[picked, bottom, first], corner.at[2, picked], (down, left)),
-            (grid.at[picked, bottom, last], corner.at[3, picked], (down, right)),
+            (grid.at[picked, first, top, :], corner.at[0, picked], (up, left)),
+            (grid.at[picked, last, top, :], corner.at[1, picked], (up, right)),
+            (grid.at[picked, first, bottom, :], corner.at[2, picked], (down, left)),
+            (grid.at[picked, last, bottom, :], corner.at[3, picked], (down, right)),
         ]
         copies = []
         for i, (source, target, device) in enumerate(plan):
@@ -248,7 +249,7 @@
     def settle(copies, first_plane, planes):
         for copy in copies:
             copy.wait()
-        beside = pl.ds(cols, LANES)
+        beside = tiles
         for plane in range(first_plane, first_plane + planes):
             from_right, from_left = unpacked[0, plane], unpacked[1, plane]
             inside = jnp.where(lane < LANES // 2, has_right.astype(jnp.int32), has_left.astype(jnp.int32)) > 0
@@ -259,53 +260,51 @@
                 if (i + 1) * SLOT < LANES:
                     tail = pltpu.roll(tail, LANES - (i + 1) * SLOT, 1)
                 joined = jnp.where(lane < LANES // 2, head, tail)
-                grid[plane, pl.ds(EDGE + i * chunk, chunk), beside] = jnp.where(inside, joined, 0.0)
+                grid[plane, beside, pl.ds(EDGE + i * chunk, chunk), :] = jnp.where(inside, joined, 0.0)
             for at, is_there, pair in ((EDGE + rows, has_down, 0), (EDGE - HALO, has_up, 2)):
                 here = pl.ds(at, HALO)
                 joined = jnp.where(edge_lane < LANES // 2, corner[pair, plane], corner[pair + 1, plane])
                 keep = jnp.where(
                     edge_lane < LANES // 2, has_right.astype(jnp.int32), has_left.astype(jnp.int32)
                 ) * is_there.astype(jnp.int32)
-                grid[plane, here, beside] = jnp.where(keep > 0, joined, 0.0)
-                every = grid[plane, here, 0:cols]
-                grid[plane, here, 0:cols] = jnp.where(is_there, every, jnp.zeros_like(every))
+                grid[plane, beside, here, :] = jnp.where(keep > 0, joined, 0.0)
+                every = grid[plane, 0:tiles, here, :]
+                grid[plane, 0:tiles, here, :] = jnp.where(is_there, every, jnp.zeros_like(every))
 
     def clear_outside():
-        beside = pl.ds(cols, LANES)
+        beside = tiles
         total = rows + 2 * HALO
         inside_lane = lax.broadcasted_iota(jnp.int32, (total, LANES), 1)
         keep = jnp.where(inside_lane < LANES // 2, has_right.astype(jnp.int32), has_left.astype(jnp.int32)) > 0
         here = pl.ds(EDGE - HALO, total)
-        grid[3, here, beside] = jnp.where(keep, grid[3, here, beside], 0.0)
+        grid[3, beside, here, :] = jnp.where(keep, grid[3, beside, here, :], 0.0)
         for at, is_there in ((EDGE + rows, has_down), (EDGE - HALO, has_up)):
             here = pl.ds(at, HALO)
-            every = grid[3, here, :]
-            grid[3, here, :] = jnp.where(is_there, every, jnp.zeros_like(every))
-
-    ring = width // LANES
+            every = grid[3, :, here, :]
+            grid[3, :, here, :] = jnp.where(is_there, every, jnp.zeros_like(every))
+
     whole = list(range(ring))
 
     def sweep_rows(body, start, total):
         step = step_of(total)
 
         def one(at):
-            around = pl.ds(pl.multiple_of(at - HALO, 8), step + 2 * HALO)
-            body(around, pl.ds(pl.multiple_of(at, 8), step), at, step)
+            body(pl.ds(pl.multiple_of(at, 8), step), at, step)
 
         if total == step:
             one(start)
         else:
             pl.loop(0, total // step)(lambda i: one(start + i * step))
 
-    def lanes(i):
-        return pl.ds(i * LANES, LANES)
-
-    def coefficients(around, here, at, step):
-        of_u = laplace(lambda i: grid[0, around, lanes(i)], step, whole, ring)
-        of_b = laplace(lambda i: grid[1, around, lanes(i)], step, whole, ring)
+    def near(ref, at, step):
+        return lambda i, shift: ref[i, pl.ds(pl.multiple_of(at, 8) + shift, step), :]
+
+    def coefficients(here, at, step):
+        of_u = laplace(near(grid.at[0], at, step), step, whole, ring)
+        of_b = laplace(near(grid.at[1], at, step), step, whole, ring)
         for (i, lap_a, mid_u), (_, lap_b, mid_b) in zip(of_u, of_b):
-            lap_u[here, lanes(i)] = lap_a
-            weight[here, lanes(i)] = OMEGA / (lap_a + lap_b + 8.0 * mid_u + 20.0 * mid_b)
+            lap_u[i, here, :] = lap_a
+            weight[i, here, :] = OMEGA / (lap_a + lap_b + 8.0 * mid_u + 20.0 * mid_b)
 
     settle(exchange(0, 3, 0), 0, 3)
     sweep_rows(coefficients, EDGE - HALO, rows + 2 * HALO)
@@ -321,25 +320,27 @@
         child = jnp.dot(
             table_row[...], jnp.concatenate(split3(wider), axis=0), preferred_element_type=jnp.float32
         )
-        grid[3, pl.ds(EDGE + j // groups_y * span, span), pl.ds(j % groups_y * span, span)] = child
+        for t in range(span // LANES):
+            here = pl.ds(EDGE + j // groups_y * span, span)
+            grid[3, j % groups_y * (span // LANES) + t, here, :] = child[:, t * LANES : (t + 1) * LANES]
 
     def first_half(tiles, start, total):
-        def body(around, here, at, step):
-            for i, of_v, mid in laplace(lambda i: grid[3, around, lanes(i)], step, tiles, ring):
-                coef = grid[0, here, lanes(i)]
-                moment[here, lanes(i)] = grid[1, here, lanes(i)] * of_v - coef * mid
-                rest[here, lanes(i)] = grid[2, here, lanes(i)] - (
-                    mid * lap_u[here, lanes(i)] - coef * of_v
+        def body(here, at, step):
+            for i, of_v, mid in laplace(near(grid.at[3], at, step), step, tiles, ring):
+                coef = grid[0, i, here, :]
+                moment[i, here, :] = grid[1, i, here, :] * of_v - coef * mid
+                rest[i, here, :] = grid[2, i, here, :] - (
+                    mid * lap_u[i, here, :] - coef * of_v
                 )
 
         sweep_rows(body, start, total)
 
     def second_half(tiles, start, total, store):
-        def body(around, here, at, step):
-            for i, of_m, _ in laplace(lambda i: moment[around, lanes(i)], step, tiles, ring):
+        def body(here, at, step):
+            for i, of_m, _ in laplace(near(moment, at, step), step, tiles, ring):
                 store(
                     at, step, here, i,
-                    grid[3, here, lanes(i)] + weight[here, lanes(i)] * (rest[here, lanes(i)] - of_m),
+                    grid[3, i, here, :] + weight[i, here, :] * (rest[i, here, :] - of_m),
                 )
 
         sweep_rows(body, start, total)
@@ -353,10 +354,10 @@
     first_half(whole, rows, strip)
 
     def keep_field(at, step, here, i, value):
-        grid[3, here, lanes(i)] = value
+        grid[3, i, here, :] = value
 
     def keep_result(at, step, here, i, value):
-        result[pl.ds(pl.multiple_of(at - EDGE, 8), step), lanes(i)] = value
+        result[i, pl.ds(pl.multiple_of(at - EDGE, 8), step), :] = value
 
     for sweep in range(SWEEPS):
         if sweep:
@@ -369,9 +370,14 @@
     for p in range(PIECES):
         second_half(whole[:-1], EDGE + p * piece, piece, keep_result)
         part = pl.ds(p * piece, piece)
-        copy = pltpu.make_async_copy(result.at[part, :], out_hbm.at[part, :], out_sem.at[p])
-        copy.start()
-        stores.append(copy)
+        for i in range(tiles):
+            copy = pltpu.make_async_copy(
+                result.at[i, part, :],
+                out_hbm.at[part, pl.ds(i * LANES, LANES)],
+                out_sem.at[p * tiles + i],
+            )
+            copy.start()
+            stores.append(copy)
     for copy in stores:
         copy.wait()
 
@@ -384,7 +390,8 @@
     rows, cols = stretch_coef.shape
     used = groups_x * groups_y + per_device
     length = -(-used // LANES) * LANES
-    full = (rows + 2 * EDGE, cols + LANES)
+    tiles = cols // LANES
+    full = (tiles + 1, rows + 2 * EDGE, LANES)
     chunk = rows * SLOT // LANES
     span = 2 * side
     f32 = jnp.float32
@@ -410,9 +417,9 @@
             pltpu.VMEM((4, 4, HALO, LANES), f32),
             pltpu.VMEM((span, 3 * side), jnp.bfloat16),
             pltpu.VMEM((3 * side, span), jnp.bfloat16),
-            pltpu.VMEM((rows, cols), f32),
+            pltpu.VMEM((tiles, rows, LANES), f32),
             pltpu.VMEM((1, length), jnp.int32),
-            dma((4,)),
+            dma((1 + 3 * tiles,)),
             dma((wide_count,)),
             dma((wide_count,)),
             dma,
@@ -420,7 +427,7 @@
             dma((wide_count,)),
             dma((2, 8)),
             dma((2, 8)),
-            dma((PIECES,)),
+            dma((PIECES * tiles,)),
         ],
         compiler_params=pltpu.CompilerParams(
             collective_id=0, has_side_effects=True, vmem_limit_bytes=52 * 1024 * 1024

time: 50 us -> 49.8 us (level)
  no operation moved by 1% of the time
where the time goes in v3:
time: 49.8 us; the launch traced here: 49.6 us
  Pallas kernels  45.1 us (91%)
  local copies, waits for them, and re-layouts  4.49 us (9%)
    pallas_call x1, Pallas kernels, local(): pl.pallas_call(functools.partial(kernel, wide_count, narrow_count, groups...  45.1 us
    unnamed x5, local copies, waits for them, and re-layouts  4.49 us

profile of v3, /device:TPU:0, one launch (start us, length us, event | category | flops | bytes accessed | tf_op | source)
XLA Modules:
  0.0 49.6 jit_solution(5300103523234621837)
XLA Ops:
  0.0 0.0 copy-start
  0.0 0.7 %copy-done = s32[2,4]{1,0:T(2,128)S(1)} copy-done((s32[2,4]{1,0:T(2,128)S(1)}, s32[2,4]{1,0:T(2,128)}, u32[]{:S(2)}) %copy-start) | copy-done | bytes 56
  0.7 0.0 copy-start.1
  0.7 0.7 %copy-done.1 = s32[32]{0:T(128)S(1)} copy-done((s32[32]{0:T(128)S(1)}, s32[32]{0:T(128)}, u32[]{:S(2)}) %copy-start.1) | copy-done | bytes 152
  1.3 45.1 %shard_map.64 = f32[512,1024]{1,0:T(8,128)} custom-call(s32[2,4]{1,0:T(2,128)S(1)} %copy-done, s32[32]{0:T(128)S(1)} %copy-done.1, f32[32,128,128]{2,1,0:T(8,128)} %old_hbm.1, f32[512,1024]{1,0:T(8,128)} %stretch_hbm.1, f32[512,1024]{1,0:T(8,128)} %bend_hbm.1, f32[512,1024]{1,0:T(8,128)} %load_hbm.1), custom_call_target="tpu_custom_call" | custom-call | tf_op jit(solution)/shard_map/pallas_call | solution.py:399
  46.5 3.2 %copy.8 = f32[512,1024]{1,0:T(8,128)} copy(f32[512,1024]{1,0:T(8,128)} %shard_map.64) | data formatting | bytes 4194304
Async XLA Ops:
  0.0 0.7 %copy-start = (s32[2,4]{1,0:T(2,128)S(1)}, s32[2,4]{1,0:T(2,128)}, u32[]{:S(2)}) copy-start(s32[2,4]{1,0:T(2,128)} %source_s.1) | copy-start | bytes 100
  0.7 0.7 %copy-start.1 = (s32[32]{0:T(128)S(1)}, s32[32]{0:T(128)}, u32[]{:S(2)}) copy-start(s32[32]{0:T(128)} %level_s.1) | copy-start | bytes 388

commit v4 on v3

--- a/solution.py
+++ b/solution.py
@@ -299,15 +299,26 @@
     def near(ref, at, step):
         return lambda i, shift: ref[i, pl.ds(pl.multiple_of(at, 8) + shift, step), :]
 
-    def coefficients(here, at, step):
-        of_u = laplace(near(grid.at[0], at, step), step, whole, ring)
-        of_b = laplace(near(grid.at[1], at, step), step, whole, ring)
-        for (i, lap_a, mid_u), (_, lap_b, mid_b) in zip(of_u, of_b):
-            lap_u[i, here, :] = lap_a
-            weight[i, here, :] = OMEGA / (lap_a + lap_b + 8.0 * mid_u + 20.0 * mid_b)
-
-    settle(exchange(0, 3, 0), 0, 3)
-    sweep_rows(coefficients, EDGE - HALO, rows + 2 * HALO)
+    def coefficients(picked, start, total):
+        def body(here, at, step):
+            of_u = laplace(near(grid.at[0], at, step), step, picked, ring)
+            of_b = laplace(near(grid.at[1], at, step), step, picked, ring)
+            for (i, lap_a, mid_u), (_, lap_b, mid_b) in zip(of_u, of_b):
+                lap_u[i, here, :] = lap_a
+                weight[i, here, :] = OMEGA / (lap_a + lap_b + 8.0 * mid_u + 20.0 * mid_b)
+
+        sweep_rows(body, start, total)
+
+    def inside(half):
+        half(whole[1:-2], 2 * EDGE, rows - 2 * EDGE)
+
+    def beside(half):
+        half(whole[-2:] + whole[:1], 2 * EDGE, rows - 2 * EDGE)
+        half(whole, EDGE - HALO, EDGE + HALO)
+        half(whole, rows, EDGE + HALO)
+
+    coef_copies = exchange(0, 3, 0)
+    inside(coefficients)
 
     for copy in parent_copies:
         copy.wait()
@@ -345,13 +356,12 @@
 
         sweep_rows(body, start, total)
 
-    strip = EDGE + HALO
-    copies = exchange(3, 1, 1)
-    first_half(whole[1:-2], 2 * EDGE, rows - 2 * EDGE)
-    settle(copies, 3, 1)
-    first_half(whole[-2:] + whole[:1], 2 * EDGE, rows - 2 * EDGE)
-    first_half(whole, EDGE - HALO, strip)
-    first_half(whole, rows, strip)
+    field_copies = exchange(3, 1, 1)
+    inside(first_half)
+    settle(coef_copies, 0, 3)
+    beside(coefficients)
+    settle(field_copies, 3, 1)
+    beside(first_half)
 
     def keep_field(at, step, here, i, value):
         grid[3, i, here, :] = value

time: 49.8 us -> 44.8 us (0.90)
  Pallas kernels: 45.1 us -> 39.7 us
    pallas_call x1, Pallas kernels: 45.1 us -> 39.7 us  [local(): pl.pallas_call(functools.partial(kernel, wide_count, narrow_count, groups...]
where the time goes in v4:
time: 44.8 us; the launch traced here: 44.2 us
  Pallas kernels  39.7 us (89%)
  local copies, waits for them, and re-layouts  4.49 us (10%)
    pallas_call x1, Pallas kernels, local(): pl.pallas_call(functools.partial(kernel, wide_count, narrow_count, groups...  39.7 us
    unnamed x5, local copies, waits for them, and re-layouts  4.49 us

profile of v4, /device:TPU:0, one launch (start us, length us, event | category | flops | bytes accessed | tf_op | source)
XLA Modules:
  0.0 44.2 jit_solution(14281985420677234709)
XLA Ops:
  0.0 0.0 copy-start
  0.0 0.7 %copy-done = s32[2,4]{1,0:T(2,128)S(1)} copy-done((s32[2,4]{1,0:T(2,128)S(1)}, s32[2,4]{1,0:T(2,128)}, u32[]{:S(2)}) %copy-start) | copy-done | bytes 56
  0.7 0.0 copy-start.1
  0.7 0.7 %copy-done.1 = s32[32]{0:T(128)S(1)} copy-done((s32[32]{0:T(128)S(1)}, s32[32]{0:T(128)}, u32[]{:S(2)}) %copy-start.1) | copy-done | bytes 152
  1.3 39.7 %shard_map.64 = f32[512,1024]{1,0:T(8,128)} custom-call(s32[2,4]{1,0:T(2,128)S(1)} %copy-done, s32[32]{0:T(128)S(1)} %copy-done.1, f32[32,128,128]{2,1,0:T(8,128)} %old_hbm.1, f32[512,1024]{1,0:T(8,128)} %stretch_hbm.1, f32[512,1024]{1,0:T(8,128)} %bend_hbm.1, f32[512,1024]{1,0:T(8,128)} %load_hbm.1), custom_call_target="tpu_custom_call" | custom-call | tf_op jit(solution)/shard_map/pallas_call | solution.py:409
  41.0 3.2 %copy.8 = f32[512,1024]{1,0:T(8,128)} copy(f32[512,1024]{1,0:T(8,128)} %shard_map.64) | data formatting | bytes 4194304
Async XLA Ops:
  0.0 0.7 %copy-start = (s32[2,4]{1,0:T(2,128)S(1)}, s32[2,4]{1,0:T(2,128)}, u32[]{:S(2)}) copy-start(s32[2,4]{1,0:T(2,128)} %source_s.1) | copy-start | bytes 100
  0.7 0.7 %copy-start.1 = (s32[32]{0:T(128)S(1)}, s32[32]{0:T(128)}, u32[]{:S(2)}) copy-start(s32[32]{0:T(128)} %level_s.1) | copy-start | bytes 388
